TPU v7x, 32 devices: a whole 2x2x4 slice. The times are simulated.
32 devices in a mesh: groups: 2 (over x), feat: 16 (over z, y, core).
Axes of the slice: x: 2, y: 2, z: 4, core: 2. Of those that a mesh axis runs over, the one named last changes fastest.
Arguments:
- samples: bfloat16 [4096, 512], P(('groups', 'feat')), parts along dimension 0, may hold values from -0.26367188 to 0.26367188
- targets: bfloat16 [4096, 256], P(('groups', 'feat')), parts along dimension 0, may hold values from -6 to 6
- frequencies: bfloat16 [512, 32768], P(None, 'feat'), may hold values from -6 to 6
- phases: float32 [32768], P('feat'), may hold values from -3.140625 to 3.140625
- coefficients: float32 [32768, 512], P('feat', 'groups'), parts along dimension 1, may hold values from -6 to 6
- eigenbasis: bfloat16 [32768, 256], P('feat', 'groups'), parts along dimension 1, may hold values from -0.03125 to 0.03125
- eigenvalues: float32 [256], P('groups'), parts along dimension 0, may hold values from 1 to 100
Outputs:
- new_coefficients: float32 [32768, 512], P('feat', 'groups'), parts along dimension 1
- scaled_projection: float32 [256, 256], P('groups'), parts along dimension 0
There are 2 independent parts, one for each index of `groups`. A program takes and returns all parts, laid end to end along the dimension named above; an argument that names none is the same for every part. Nothing has to cross between parts.
All inputs are finite; a program needn't handle non-finite values.
Results may differ from a plain program's by a relative error of at most 0.005.
Values may be sent and summed in bfloat16 or wider, within the bound.
A program may use at most 128 MiB of HBM per device.

v0:
```python
import jax
import jax.numpy as jnp
from jax import lax
from jax.sharding import PartitionSpec as P

STEPS = 2


def split_parts(values):
    upper = values.astype(jnp.bfloat16)
    lower = (values - upper.astype(jnp.float32)).astype(jnp.bfloat16)
    return (upper, lower)


def left_product(matrix, values):
    upper, lower = split_parts(values)
    dims = (((0,), (0,)), ((), ()))
    first = lax.dot_general(matrix, upper, dims, preferred_element_type=jnp.float32)
    return first + lax.dot_general(matrix, lower, dims, preferred_element_type=jnp.float32)


def right_product(matrix, values):
    upper, lower = split_parts(values)
    first = jnp.dot(matrix, upper, preferred_element_type=jnp.float32)
    return first + jnp.dot(matrix, lower, preferred_element_type=jnp.float32)


def local(samples, targets, frequencies, phases, coefficients, eigenbasis, eigenvalues):
    rows_dev = samples.shape[0]
    feat_dev = frequencies.shape[1]
    group_size = lax.axis_size("feat")
    total_rows = rows_dev * group_size
    total_feat = feat_dev * group_size
    offset_feat = lax.axis_index("feat") * feat_dev
    index = (offset_feat + jnp.arange(feat_dev, dtype=jnp.int32)).astype(jnp.float32)
    sweep = jnp.exp(jnp.log(8.0) * index / total_feat)
    product = jnp.dot(
        lax.all_gather(samples, "feat", axis=0, tiled=True),
        frequencies,
        preferred_element_type=jnp.float32,
    )
    features = jnp.cos(product * sweep[None, :] + phases[None, :]).astype(jnp.bfloat16)
    retained = 1.0 - 1.0 / eigenvalues
    step_rate = 0.5 * jnp.sqrt(jnp.float32(total_rows) / jnp.float32(total_feat))
    feature_norm = 1.0 / jnp.sqrt(jnp.float32(total_feat))
    sample_norm = 1.0 / jnp.sqrt(jnp.float32(total_rows))
    whole_targets = lax.all_gather(targets, "feat", axis=0, tiled=True)
    current = coefficients
    scaled = jnp.zeros((eigenbasis.shape[1], coefficients.shape[1]), jnp.float32)
    for iteration in range(STEPS):
        current_low = current.astype(jnp.bfloat16)
        partial_sum = (
            jnp.dot(features, current_low, preferred_element_type=jnp.float32) * feature_norm
        )
        prediction = lax.psum(partial_sum, "feat")
        residual = (prediction - whole_targets.astype(jnp.float32)).astype(jnp.bfloat16)
        gradient = (
            lax.dot_general(
                features, residual, (((0,), (0,)), ((), ())), preferred_element_type=jnp.float32
            )
            * sample_norm
        )
        local_part = left_product(eigenbasis, gradient)
        projected = lax.psum(local_part, "feat")
        scaled = retained[:, None] * projected
        correction = right_product(eigenbasis, scaled)
        current = current - step_rate * (gradient - correction)
    return (current, scaled)


def solution(mesh):
    return jax.shard_map(
        local,
        mesh=mesh,
        in_specs=(
            P(("groups", "feat"), None),
            P(("groups", "feat"), None),
            P(None, "feat"),
            P("feat"),
            P("feat", "groups"),
            P("feat", "groups"),
            P("groups"),
        ),
        out_specs=(P("feat", "groups"), P("groups", None)),
        check_vma=False,
    )
```

profile of v0, /device:TPU:1, one launch (start us, length us, event | category | flops | bytes accessed | tf_op | source)
XLA Modules:
  0.0 532.4 jit_solution(14496162181707475414)
XLA Ops:
  7.2 0.0 copy-start
  7.2 0.0 all-gather.3.cloned.1.call-start
  7.2 0.7 all-gather.3.cloned.1.call-update
  7.9 0.0 all-gather.5.cloned.1.call-start
  8.0 0.7 all-gather.5.cloned.1.call-update
  8.7 0.0 all-reduce.5.cloned.1.call-start
  8.7 45.4 %all-gather.3.cloned.1.call-done = bf16[2048,512]{1,0:T(8,128)(2,1)} async-done(((bf16[128,512]{1,0:T(8,128)(2,1)}), bf16[2048,512]{1,0:T(8,128)(2,1)}) %all-gather.3.cloned.1.call-update) | async-done | bytes 2097168 | tf_op jit(solution)/shard_map/all_gather | solution.py:38
  54.1 0.0 copy-done
  54.1 60.0 %cosine_convert_fusion = bf16[2048,2048]{1,0:T(8,128)(2,1)S(1)} fusion(bf16[2048,512]{1,0:T(8,128)(2,1)} %all-gather.3.cloned.1.call-done, bf16[512,2048]{1,0:T(8,128)(2,1)S(1)} %copy-done, f32[2048]{0:T(1024)} %param.10, f32[2048]{0:T(1024)S(1)} %multiply_exponential_fusion), kind=kOutput, calls=%fused_computation | convolution fusion | flops 4307550208 | bytes 12599296 | tf_op jit(solution)/shard_map/dot_general | solution.py:37
  114.1 3.2 copy-done.10
  117.3 0.0 copy-done.7
  117.3 3.8 convolution_multiply_fusion.3
  121.1 0.0 all-reduce.5.cloned.1.call-update
  121.1 0.0 copy-start.1
  121.1 0.0 all-reduce.7.cloned.1.call-start
  121.2 0.0 all-gather.5.cloned.1.call-done
  121.2 95.4 %all-reduce.5.cloned.1.call-done = f32[2048,256]{1,0:T(8,128)} async-done(((f32[2048,256]{1,0:T(8,128)}), f32[2048,256]{1,0:T(8,128)}) %all-reduce.5.cloned.1.call-update) | async-done | bytes 2097168 | tf_op jit(solution)/shard_map/psum | solution.py:55
  216.6 6.8 %convolution_multiply_fusion.2 = f32[2048,256]{1,0:T(8,128)S(1)} fusion(bf16[2048,2048]{1,0:T(8,128)(2,1)} %copy-done.10, f32[2048,256]{1,0:T(8,128)} %all-reduce.5.cloned.1.call-done, bf16[2048,256]{1,0:T(8,128)(2,1)} %all-gather.5.cloned.1.call-done), kind=kOutput, calls=%fused_computation.3 | convolution fusion | flops 2149580800 | bytes 13631488 | tf_op jit(solution)/shard_map/dot_general | solution.py:58
  223.4 0.0 copy-start.4
  223.4 0.5 fusion.20
  223.9 0.8 copy-done.4
  224.7 1.1 fusion.11
  225.9 0.0 all-reduce.7.cloned.1.call-update
  225.9 0.2 all-reduce.9.cloned.1.call-start
  226.1 87.4 %all-reduce.7.cloned.1.call-done = f32[128,256]{0,1:T(8,128)} async-done(((f32[128,256]{0,1:T(8,128)}), f32[128,256]{0,1:T(8,128)}) %all-reduce.7.cloned.1.call-update) | async-done | bytes 131088 | tf_op jit(solution)/shard_map/psum | solution.py:64
  313.5 1.5 fusion.22
  315.0 0.2 copy-done.5
  315.2 0.0 copy-done.8
  315.2 2.3 fusion.7
  317.4 0.0 copy-start.6
  317.5 1.3 copy-done.6
  318.8 1.2 copy-done.11
  319.9 3.8 convolution_multiply_fusion.1
  323.7 0.0 all-reduce.9.cloned.1.call-update
  323.7 0.0 all-reduce.11.cloned.1.call-start
  323.8 98.2 %all-reduce.9.cloned.1.call-done = f32[2048,256]{1,0:T(8,128)} async-done(((f32[2048,256]{1,0:T(8,128)}), f32[2048,256]{1,0:T(8,128)}) %all-reduce.9.cloned.1.call-update) | async-done | bytes 2097168 | tf_op jit(solution)/shard_map/psum | solution.py:55
  422.0 6.8 %convolution_multiply_fusion = f32[2048,256]{1,0:T(8,128)S(1)} fusion(bf16[2048,2048]{1,0:T(8,128)(2,1)} %copy-done.10, f32[2048,256]{1,0:T(8,128)} %all-reduce.9.cloned.1.call-done, bf16[2048,256]{1,0:T(8,128)(2,1)} %all-gather.5.cloned.1.call-done), kind=kOutput, calls=%fused_computation.1 | convolution fusion | flops 2149580800 | bytes 13631488 | tf_op jit(solution)/shard_map/dot_general | solution.py:58
  428.7 0.0 copy-start.2
  428.8 0.5 fusion.17
  429.2 0.8 copy-done.2
  430.1 1.1 fusion.10
  431.2 0.0 all-reduce.11.cloned.1.call-update
  431.2 87.6 %all-reduce.11.cloned.1.call-done = f32[128,256]{0,1:T(8,128)} async-done(((f32[128,256]{0,1:T(8,128)}), f32[128,256]{0,1:T(8,128)}) %all-reduce.11.cloned.1.call-update) | async-done | bytes 131088 | tf_op jit(solution)/shard_map/psum | solution.py:64
  518.9 0.9 broadcast_multiply_fusion
  519.8 0.8 copy.13
  520.6 0.4 fusion.26
  521.0 1.2 copy-done.3
  522.1 3.4 fusion.3
  (11 shorter events, 0.0 us)
Async XLA Ops:
  7.2 46.9 %copy-start = (bf16[512,2048]{1,0:T(8,128)(2,1)S(1)}, bf16[512,2048]{1,0:T(8,128)(2,1)}, u32[]{:S(2)}) copy-start(bf16[512,2048]{1,0:T(8,128)(2,1)} %param.9) | copy-start | bytes 6291460
  7.2 46.9 %all-gather.3.cloned.1.call-start = ((), (), s32[]{:S(2)}) async-start(), calls=%async_computation | async-start | bytes 2228224 | tf_op jit(solution)/shard_map/all_gather | solution.py:38
  7.9 113.3 %all-gather.5.cloned.1.call-start = ((), (), s32[]{:S(2)}) async-start(), calls=%async_computation.2 | async-start | bytes 1114112 | tf_op jit(solution)/shard_map/all_gather | solution.py:47
  8.7 207.9 %all-reduce.5.cloned.1.call-start = ((), (), s32[]{:S(2)}) async-start(), calls=%async_computation.1 | async-start | bytes 4194304 | tf_op jit(solution)/shard_map/psum | solution.py:55
  54.1 63.2 %copy-start.7 = (f32[2048,256]{1,0:T(8,128)S(1)}, f32[2048,256]{1,0:T(8,128)}, u32[]{:S(2)}) copy-start(f32[2048,256]{1,0:T(8,128)} %param.11) | copy-start | bytes 6291460
  114.1 3.2 copy-start.10
  121.1 102.3 %copy-start.1 = (bf16[2048,128]{1,0:T(8,128)(2,1)S(1)}, bf16[2048,128]{1,0:T(8,128)(2,1)}, u32[]{:S(2)}) copy-start(bf16[2048,128]{1,0:T(8,128)(2,1)} %param.12) | copy-start | bytes 1572868
  121.1 192.4 %all-reduce.7.cloned.1.call-start = ((), (), s32[]{:S(2)}) async-start(), calls=%async_computation.3 | async-start | bytes 262144 | tf_op jit(solution)/shard_map/psum | solution.py:64
  223.4 1.3 copy-start.4
  224.7 1.4 copy-start.9
  225.9 196.1 %all-reduce.9.cloned.1.call-start = ((), (), s32[]{:S(2)}) async-start(), calls=%async_computation.4 | async-start | bytes 4194304 | tf_op jit(solution)/shard_map/psum | solution.py:55
  313.5 1.7 copy-start.5
  313.5 1.7 copy-start.8
  315.2 4.8 copy-start.11
  317.4 1.3 copy-start.6
  323.7 195.1 %all-reduce.11.cloned.1.call-start = ((), (), s32[]{:S(2)}) async-start(), calls=%async_computation.5 | async-start | bytes 262144 | tf_op jit(solution)/shard_map/psum | solution.py:64
  428.7 1.3 copy-start.2
  520.6 1.6 copy-start.3
Sparse Core Ops, SparseCore 0:
  10.2 43.8 all-gather.2
  56.3 36.7 all-gather.4
  121.3 95.3 all-reduce.4
  226.0 87.4 all-reduce.6
  323.9 98.0 all-reduce.8
  431.4 87.4 all-reduce.10
where the time goes:
time: 534 us; the launch traced here: 532 us
  waiting for transfers between devices  415 us (78%)
  matrix products  91.9 us (17%)
  between operations  14.3 us (3%)
  local copies, waits for them, and re-layouts  9.5 us (2%)
    psum x2, waiting for transfers between devices, local(): prediction = lax.psum(partial_sum, 'feat')  194 us
    psum x2, waiting for transfers between devices, local(): projected = lax.psum(local_part, 'feat')  175 us
    dot_general x1, matrix products, local(): jnp.dot(lax.all_gather(samples, 'feat', axis=0, tiled=True), frequencies,...  60 us
    all_gather x1, waiting for transfers between devices, local(): lax.all_gather(samples, 'feat', axis=0, tiled=True)  45.4 us
    dot_general x2, matrix products, local(): lax.dot_general(features, residual, (((0,), (0,)), ((), ())), preferred_e...  13.5 us
  transfers between devices with their start and end apart: 6, of which 5 were waited for; matrix products, arithmetic and copies ran while one was open for 12% of the time, Pallas kernels for 0%

commit v1 on v0

v1 whole, which is shorter than its diff:
```python
import functools
import math

import jax
import jax.numpy as jnp
from jax import lax
from jax.experimental import pallas as pl
from jax.experimental.pallas import tpu as pltpu
from jax.sharding import PartitionSpec as P

STEPS = 2
F32 = jnp.float32
BF16 = jnp.bfloat16
COSINE = (
    0.9999991998413434, -19.738978175861273, 64.92858783993262,
    -85.27084362689533, 58.786940762944745, -21.065429407375632,
)
TN_DIMS = (((0,), (0,)), ((), ()))


def tn_dot(left, right):
    return lax.dot_general(left, right, TN_DIMS, preferred_element_type=F32)


class Gather:
    def __init__(self, place, buf, rows, recv, send):
        self.place, self.buf, self.rows, self.recv, self.send = place, buf, rows, recv, send

    def copy(self, chunk, slot, target):
        part = self.buf.at[pl.ds(pl.multiple_of(chunk * self.rows, self.rows), self.rows)]
        return pltpu.make_async_remote_copy(
            src_ref=part,
            dst_ref=part,
            send_sem=self.send.at[slot],
            recv_sem=self.recv.at[chunk],
            device_id={"feat": target},
            device_id_type=pl.DeviceIdType.MESH,
        )

    def arrived(self, chunk):
        self.copy(chunk, 0, self.place.sibling).wait_recv()

    def line_copies(self, k):
        s = self.place
        chunk = s.chunk(k, s.y, s.c)
        right = (s.q + 1 < s.zn) if k == 0 else jnp.logical_and(s.order[k] < s.q, s.q + 1 < s.zn)
        left = (s.q > 0) if k == 0 else jnp.logical_and(s.order[k] > s.q, s.q > 0)
        return (
            (right, self.copy(chunk, 5 * k, s.device(jnp.minimum(s.q + 1, s.zn - 1), s.y, s.c))),
            (left, self.copy(chunk, 5 * k + 1, s.device(jnp.maximum(s.q - 1, 0), s.y, s.c))),
        )

    def near_copies(self, k):
        s = self.place
        chunk = s.chunk(k, s.y, s.c)
        return (self.copy(chunk, 5 * k + 2, s.partner), self.copy(chunk, 5 * k + 3, s.sibling))

    def cross_copy(self, k):
        s = self.place
        return self.copy(s.chunk(k, 1 - s.y, s.c), 5 * k + 4, s.sibling)

    def forward(self, k):
        s = self.place
        if k > 0:
            self.arrived(s.chunk(k, s.y, s.c))
        for needed, copy in self.line_copies(k):
            pl.when(needed)(copy.start)
        for copy in self.near_copies(k):
            copy.start()

    def cross(self, k):
        s = self.place
        self.arrived(s.chunk(k, 1 - s.y, s.c))
        self.cross_copy(k).start()

    def near_half(self, k):
        s = self.place
        self.arrived(s.chunk(k, s.y, 1 - s.c))

    def far_half(self, k):
        s = self.place
        self.arrived(s.chunk(k, 1 - s.y, 1 - s.c))

    def finish(self):
        for k in range(self.place.zn):
            for needed, copy in self.line_copies(k):
                pl.when(needed)(copy.wait_send)
            for copy in self.near_copies(k):
                copy.wait_send()
            self.cross_copy(k).wait_send()


class Scatter:
    def __init__(self, place, rows, keep, core, side, line, core_sem, side_sem, line_sem):
        self.place, self.rows = place, rows
        self.keep = keep
        self.core_out, self.core_in = core
        self.side_out, self.side_in = side
        self.line_out, self.line_in = line
        self.core_sem, self.side_sem, self.line_sem = core_sem, side_sem, line_sem

    def core_copy(self, slot):
        return pltpu.make_async_remote_copy(
            src_ref=self.core_out.at[slot],
            dst_ref=self.core_in.at[slot],
            send_sem=self.core_sem.at[0, slot],
            recv_sem=self.core_sem.at[1, slot],
            device_id={"feat": self.place.sibling},
            device_id_type=pl.DeviceIdType.MESH,
        )

    def side_copy(self, k):
        return pltpu.make_async_remote_copy(
            src_ref=self.side_out.at[k],
            dst_ref=self.side_in.at[k],
            send_sem=self.side_sem.at[0, k],
            recv_sem=self.side_sem.at[1, k],
            device_id={"feat": self.place.partner},
            device_id_type=pl.DeviceIdType.MESH,
        )

    def line_copy(self, k):
        s = self.place
        return pltpu.make_async_remote_copy(
            src_ref=self.line_out.at[k],
            dst_ref=self.line_in.at[s.q],
            send_sem=self.line_sem.at[0, k],
            recv_sem=self.line_sem.at[1, s.q],
            device_id={"feat": s.device(s.order[k], s.y, s.c)},
            device_id_type=pl.DeviceIdType.MESH,
        )

    def line_arrival(self, k):
        s = self.place
        other = s.order[k]
        return pltpu.make_async_remote_copy(
            src_ref=self.line_out.at[k],
            dst_ref=self.line_in.at[other],
            send_sem=self.line_sem.at[0, k],
            recv_sem=self.line_sem.at[1, other],
            device_id={"feat": s.device(other, s.y, s.c)},
            device_id_type=pl.DeviceIdType.MESH,
        )

    def put(self, k, far, sums):
        slot = 2 * k + far
        self.keep[slot] = sums(self.place.c)
        self.core_out[slot] = sums(1 - self.place.c).astype(BF16)
        self.core_copy(slot).start()

    def merge_core(self, k, far):
        slot = 2 * k + far
        self.core_copy(slot).wait_recv()
        total = self.keep[slot] + self.core_in[slot].astype(F32)
        if far:
            self.side_out[k] = total.astype(BF16)
            self.side_copy(k).start()
        else:
            self.keep[slot] = total

    def merge_side(self, k):
        self.side_copy(k).wait_recv()
        total = self.keep[2 * k] + self.side_in[k].astype(F32)
        if k:
            self.line_out[k] = total.astype(BF16)
            self.line_copy(k).start()
        else:
            self.keep[0] = total

    def result(self):
        total = self.keep[0]
        for k in range(1, self.place.zn):
            self.line_arrival(k).wait_recv()
            total = total + self.line_in[self.place.order[k]].astype(F32)
        return total

    def finish(self):
        for k in range(self.place.zn):
            self.core_copy(2 * k).wait_send()
            self.core_copy(2 * k + 1).wait_send()
            self.side_copy(k).wait_send()
            if k:
                self.line_copy(k).wait_send()


class Place:
    def __init__(self, size):
        self.zn = zn = size // 4
        me = lax.axis_index("feat")
        self.me = me
        self.q = q = me // 4
        self.y = (me // 2) % 2
        self.c = me % 2
        near = jnp.minimum(q, zn - 1 - q)
        self.order = []
        for k in range(zn):
            step = -((k + 1) // 2) if k % 2 else k // 2
            edge = jnp.where(q == near, k, zn - 1 - k)
            self.order.append(jnp.where(k <= 2 * near, q + step, edge))
        self.sibling = self.device(q, self.y, 1 - self.c)
        self.partner = self.device(q, 1 - self.y, self.c)

    def device(self, q, y, c):
        return (q * 2 + y) * 2 + c

    def chunk(self, k, y, c):
        return self.device(self.order[k], y, c)


def kernel(
    size, total_feat,
    x_ref, y_ref, w_ref, phase_ref, a_ref, e_ref, eig_ref,
    out_ref, scaled_ref,
    xs, feats, spread, joint, low, grad, part, res1, res2,
    keep1, core_out1, core_in1, side_out1, side_in1, line_out1, line_in1,
    keep2, core_out2, core_in2, side_out2, side_in2, line_out2, line_in2,
    g_recv, g_send, s_core, s_side, s_line,
):
    place = Place(size)
    zn = place.zn
    rows = x_ref.shape[0]
    feat_dev = w_ref.shape[1]
    outs = a_ref.shape[1]
    top = e_ref.shape[1]
    tile = min(256, feat_dev)
    tiles = feat_dev // tile
    total_rows = rows * size
    step_rate = 0.5 * math.sqrt(total_rows / total_feat)
    feature_norm = 1.0 / math.sqrt(total_feat)
    sample_norm = 1.0 / math.sqrt(total_rows)

    barrier = pltpu.get_barrier_semaphore()
    others = [place.sibling, place.partner] + [
        place.device(place.order[k], place.y, place.c) for k in range(1, zn)
    ]
    for other in others:
        pl.semaphore_signal(
            barrier, inc=1, device_id={"feat": other}, device_id_type=pl.DeviceIdType.MESH
        )

    own = pl.ds(pl.multiple_of(place.me * rows, rows), rows)
    xs[own, :] = x_ref[...]
    pl.semaphore_wait(barrier, len(others))
    gather_x = Gather(place, xs, rows, g_recv.at[0], g_send.at[0])
    gather_x.forward(0)

    index = (place.me * feat_dev + lax.broadcasted_iota(jnp.int32, (8, feat_dev), 1)).astype(F32)
    turn = 1.0 / (2.0 * math.pi)
    sweep = jnp.exp(F32(math.log(8.0)) * index / F32(total_feat))
    spread[0:8, :] = sweep * turn
    spread[8:16, :] = jnp.broadcast_to(phase_ref[...] * turn, (8, feat_dev))
    joint[:, :outs] = a_ref[...].astype(BF16)
    joint[:, outs:] = e_ref[...]

    pair = 2 * rows

    def pair_rows(k, far):
        y = 1 - place.y if far else place.y
        first = (place.order[k] * 2 + y) * pair
        return pl.ds(pl.multiple_of(first, pair), pair)

    def make_features(span):
        def body(i, carry):
            cols = pl.ds(pl.multiple_of(i * tile, tile), tile)
            product = jnp.dot(xs[span, :], w_ref[:, cols], preferred_element_type=F32)
            turns = product * spread[0:1, cols] + spread[8:9, cols]
            f = turns - jnp.round(turns)
            u = f * f
            value = jnp.full_like(u, COSINE[-1])
            for coefficient in COSINE[-2::-1]:
                value = value * u + coefficient
            feats[span, cols] = value.astype(BF16)
            return carry

        lax.fori_loop(0, tiles, body, 0, unroll=2)

    def predict(span, factors, scatter, k, far, columns):
        part[:, :columns] = jnp.dot(feats[span, :], factors[...], preferred_element_type=F32)

        def sums(core):
            return part[pl.ds(pl.multiple_of(core * rows, rows), rows), :columns]

        scatter.put(k, far, sums)

    scatter1 = Scatter(
        place, rows, keep1, (core_out1, core_in1), (side_out1, side_in1), (line_out1, line_in1),
        s_core.at[0], s_side.at[0], s_line.at[0],
    )
    scatter2 = Scatter(
        place, rows, keep2, (core_out2, core_in2), (side_out2, side_in2), (line_out2, line_in2),
        s_core.at[1], s_side.at[1], s_line.at[1],
    )

    for k in range(zn):
        gather_x.near_half(k)
        make_features(pair_rows(k, 0))
        gather_x.cross(k)
        if k + 1 < zn:
            gather_x.forward(k + 1)
        predict(pair_rows(k, 0), joint, scatter1, k, 0, outs + top)
        if k:
            scatter1.merge_core(k - 1, 1)
        gather_x.far_half(k)
        make_features(pair_rows(k, 1))
        scatter1.merge_core(k, 0)
        predict(pair_rows(k, 1), joint, scatter1, k, 1, outs + top)
        if k:
            scatter1.merge_side(k - 1)
    scatter1.merge_core(zn - 1, 1)
    scatter1.merge_side(zn - 1)

    total = scatter1.result()
    prediction = total[:, :outs] * feature_norm
    res1[own, :outs] = (prediction - y_ref[...].astype(F32)).astype(BF16)
    res1[own, outs:] = total[:, outs:].astype(BF16)

    eig = jnp.broadcast_to(1.0 - 1.0 / eig_ref[...], (top, top))
    same = lax.broadcasted_iota(jnp.int32, (top, top), 0) == lax.broadcasted_iota(
        jnp.int32, (top, top), 1
    )
    retained = jnp.sum(jnp.where(same, eig, 0.0), axis=1, keepdims=True)

    def descend(gather, res, source):
        quad = 4 * rows
        projected = jnp.zeros((top, outs), F32)
        gather.forward(0)
        for k in range(zn):
            gather.cross(k)
            if k + 1 < zn:
                gather.forward(k + 1)
            gather.near_half(k)
            gather.far_half(k)
            span = pl.ds(pl.multiple_of(place.order[k] * quad, quad), quad)

            def body(i, carry):
                cols = pl.ds(pl.multiple_of(i * tile, tile), tile)
                term = tn_dot(feats[span, cols], res[span, :outs])
                grad[cols, :] = term if k == 0 else grad[cols, :] + term
                return carry

            lax.fori_loop(0, tiles, body, 0)
            projected = projected + tn_dot(res1[span, outs:], res[span, :outs])
        scaled = retained * (projected * sample_norm)
        upper = scaled.astype(BF16)
        lower = (scaled - upper.astype(F32)).astype(BF16)

        def update(i, carry):
            cols = pl.ds(pl.multiple_of(i * tile, tile), tile)
            basis = e_ref[cols, :]
            correction = jnp.dot(basis, upper, preferred_element_type=F32) + jnp.dot(
                basis, lower, preferred_element_type=F32
            )
            new = source[cols, :] - step_rate * (grad[cols, :] * sample_norm - correction)
            out_ref[cols, :] = new
            low[cols, :] = new.astype(BF16)
            return carry

        lax.fori_loop(0, tiles, update, 0)
        return scaled

    gather1 = Gather(place, res1, rows, g_recv.at[1], g_send.at[1])
    descend(gather1, res1, a_ref)

    for k in reversed(range(zn)):
        for far in (1, 0):
            predict(pair_rows(k, far), low, scatter2, k, far, outs)
        if k + 1 < zn:
            scatter2.merge_core(k + 1, 1)
            scatter2.merge_core(k + 1, 0)
        if k + 2 < zn:
            scatter2.merge_side(k + 2)
    scatter2.merge_core(0, 1)
    scatter2.merge_core(0, 0)
    scatter2.merge_side(1)
    scatter2.merge_side(0)
    prediction = scatter2.result() * feature_norm
    res2[own, :] = (prediction - y_ref[...].astype(F32)).astype(BF16)
    gather2 = Gather(place, res2, rows, g_recv.at[2], g_send.at[2])
    scaled_ref[...] = descend(gather2, res2, out_ref)

    for transfer in (gather_x, scatter1, gather1, scatter2, gather2):
        transfer.finish()


def local(samples, targets, frequencies, phases, coefficients, eigenbasis, eigenvalues):
    size = lax.axis_size("feat")
    rows, din = samples.shape
    feat_dev = frequencies.shape[1]
    outs = coefficients.shape[1]
    top = eigenbasis.shape[1]
    zn = size // 4
    wide = outs + top
    total_rows = rows * size

    def scatter_buffers(columns):
        return [
            pltpu.VMEM((2 * zn, rows, columns), F32),
            pltpu.VMEM((2 * zn, rows, columns), BF16),
            pltpu.VMEM((2 * zn, rows, columns), BF16),
            pltpu.VMEM((zn, rows, columns), BF16),
            pltpu.VMEM((zn, rows, columns), BF16),
            pltpu.VMEM((zn, rows, columns), BF16),
            pltpu.VMEM((zn, rows, columns), BF16),
        ]

    vmem = pl.BlockSpec(memory_space=pltpu.VMEM)
    return pl.pallas_call(
        functools.partial(kernel, size, feat_dev * size),
        out_shape=(
            jax.ShapeDtypeStruct(coefficients.shape, F32),
            jax.ShapeDtypeStruct((top, outs), F32),
        ),
        in_specs=[vmem] * 7,
        out_specs=(vmem, vmem),
        scratch_shapes=[
            pltpu.VMEM((total_rows, din), BF16),
            pltpu.VMEM((total_rows, feat_dev), BF16),
            pltpu.VMEM((16, feat_dev), F32),
            pltpu.VMEM((feat_dev, wide), BF16),
            pltpu.VMEM((feat_dev, outs), BF16),
            pltpu.VMEM((feat_dev, outs), F32),
            pltpu.VMEM((2 * rows, wide), F32),
            pltpu.VMEM((total_rows, wide), BF16),
            pltpu.VMEM((total_rows, outs), BF16),
            *scatter_buffers(wide),
            *scatter_buffers(outs),
            pltpu.SemaphoreType.DMA((3, size)),
            pltpu.SemaphoreType.DMA((3, 5 * zn)),
            pltpu.SemaphoreType.DMA((2, 2, 2 * zn)),
            pltpu.SemaphoreType.DMA((2, 2, zn)),
            pltpu.SemaphoreType.DMA((2, 2, zn)),
        ],
        compiler_params=pltpu.CompilerParams(
            collective_id=0, has_side_effects=True, vmem_limit_bytes=60 * 1024 * 1024
        ),
    )(
        samples, targets, frequencies, phases.reshape(1, feat_dev), coefficients, eigenbasis,
        eigenvalues.reshape(1, top),
    )


def solution(mesh):
    return jax.shard_map(
        local,
        mesh=mesh,
        in_specs=(
            P(("groups", "feat"), None),
            P(("groups", "feat"), None),
            P(None, "feat"),
            P("feat"),
            P("feat", "groups"),
            P("feat", "groups"),
            P("groups"),
        ),
        out_specs=(P("feat", "groups"), P("groups", None)),
        check_vma=False,
    )
```

time: 534 us -> 124 us (0.23)
  waiting for transfers between devices: 415 us -> 0 us
  Pallas kernels: 0 us -> 119 us
  matrix products: 91.9 us -> 0 us
  between operations: 14.3 us -> 0.65 us
  local copies, waits for them, and re-layouts: 9.5 us -> 3.74 us
    psum x4 -> x0, waiting for transfers between devices: 369 us -> none  [the longest x2 194 us: local(): prediction = lax.psum(partial_sum, 'feat')]
    pallas_call x0 -> x1, Pallas kernels: none -> 119 us  [local(): pl.pallas_call(functools.partial(kernel, size, feat_dev * size), out_shap...]
    dot_general x13 -> x0, matrix products: 91.9 us -> none  [the longest x1 60 us: local(): jnp.dot(lax.all_gather(samples, 'feat', axis=0, tiled=True), frequencies,...]
    all_gather x2 -> x0, waiting for transfers between devices: 45.4 us -> none  [the longest x1 45.4 us: local(): lax.all_gather(samples, 'feat', axis=0, tiled=True)]
    unnamed x25 -> x4, local copies, waits for them, and re-layouts: 9.5 us -> 3.74 us
  transfers between devices with their start and end apart: 6 -> 0, of which waited for: 5 -> 0; matrix products, arithmetic and copies ran while one was open for 12% -> 0% of each run, Pallas kernels for 0% -> 0%
where the time goes in v1:
time: 124 us; the launch traced here: 123 us
  Pallas kernels  119 us (96%)
  local copies, waits for them, and re-layouts  3.74 us (3%)
    pallas_call x1, Pallas kernels, local(): pl.pallas_call(functools.partial(kernel, size, feat_dev * size), out_shap...  119 us
    unnamed x4, local copies, waits for them, and re-layouts  3.74 us

profile of v1, /device:TPU:1, one launch (start us, length us, event | category | flops | bytes accessed | tf_op | source)
XLA Modules:
  0.0 123.2 jit_solution(11832699116529218455)
XLA Ops:
  0.6 118.8 %shard_map.86 = (f32[2048,256]{1,0:T(8,128)}, f32[128,256]{1,0:T(8,128)}) custom-call(bf16[128,512]{1,0:T(8,128)(2,1)} %x_ref.1, bf16[128,256]{1,0:T(8,128)(2,1)} %y_ref.1, bf16[512,2048]{1,0:T(8,128)(2,1)} %w_ref.1, f32[1,2048]{1,0:T(1,128)} %bitcast.2, f32[2048,256]{1,0:T(8,128)} %a_ref.1, bf16[2048,128]{1,0:T(8,128)(2,1)} %e_ref.1, f32[1,128]{1,0:T(1,128)} %bitcast.3), custom_call_target="tpu_custom_call" | custom-call | tf_op jit(solution)/shard_map/pallas_call | solution.py:407
  119.5 0.0 copy-start
  119.5 3.1 %copy.11 = f32[2048,256]{1,0:T(8,128)} copy(f32[2048,256]{1,0:T(8,128)} %get-tuple-element.4) | data formatting | bytes 4194304
  122.6 0.0 copy-done
  122.6 0.7 copy.12
Async XLA Ops:
  119.5 3.1 %copy-start = (f32[128,256]{1,0:T(8,128)S(1)}, f32[128,256]{1,0:T(8,128)}, u32[]{:S(2)}) copy-start(f32[128,256]{1,0:T(8,128)} %get-tuple-element.5) | copy-start | bytes 393220

commit v2 on v1

--- a/solution.py
+++ b/solution.py
@@ -272,7 +272,7 @@
             feats[span, cols] = value.astype(BF16)
             return carry
 
-        lax.fori_loop(0, tiles, body, 0, unroll=2)
+        lax.fori_loop(0, tiles, body, 0, unroll=True)
 
     def predict(span, factors, scatter, k, far, columns):
         part[:, :columns] = jnp.dot(feats[span, :], factors[...], preferred_element_type=F32)
@@ -338,7 +338,7 @@
                 grad[cols, :] = term if k == 0 else grad[cols, :] + term
                 return carry
 
-            lax.fori_loop(0, tiles, body, 0)
+            lax.fori_loop(0, tiles, body, 0, unroll=True)
             projected = projected + tn_dot(res1[span, outs:], res[span, :outs])
         scaled = retained * (projected * sample_norm)
         upper = scaled.astype(BF16)

time: 124 us -> 115 us (0.927)
  Pallas kernels: 119 us -> 110 us
    pallas_call x1, Pallas kernels: 119 us -> 110 us  [local(): pl.pallas_call(functools.partial(kernel, size, feat_dev * size), out_shap...]
where the time goes in v2:
time: 115 us
  Pallas kernels  110 us (96%)
  local copies, waits for them, and re-layouts  3.74 us (3%)
    pallas_call x1, Pallas kernels, local(): pl.pallas_call(functools.partial(kernel, size, feat_dev * size), out_shap...  110 us
    unnamed x4, local copies, waits for them, and re-layouts  3.74 us

profile of v2, /device:TPU:1, one launch (start us, length us, event | category | flops | bytes accessed | tf_op | source)
XLA Modules:
  0.0 114.5 jit_solution(5443611864361832580)
XLA Ops:
  0.6 110.1 %shard_map.86 = (f32[2048,256]{1,0:T(8,128)}, f32[128,256]{1,0:T(8,128)}) custom-call(bf16[128,512]{1,0:T(8,128)(2,1)} %x_ref.1, bf16[128,256]{1,0:T(8,128)(2,1)} %y_ref.1, bf16[512,2048]{1,0:T(8,128)(2,1)} %w_ref.1, f32[1,2048]{1,0:T(1,128)} %bitcast.2, f32[2048,256]{1,0:T(8,128)} %a_ref.1, bf16[2048,128]{1,0:T(8,128)(2,1)} %e_ref.1, f32[1,128]{1,0:T(1,128)} %bitcast.3), custom_call_target="tpu_custom_call" | custom-call | tf_op jit(solution)/shard_map/pallas_call | solution.py:407
  110.8 0.0 copy-start
  110.8 3.1 %copy.11 = f32[2048,256]{1,0:T(8,128)} copy(f32[2048,256]{1,0:T(8,128)} %get-tuple-element.4) | data formatting | bytes 4194304
  113.8 0.0 copy-done
  113.8 0.7 copy.12
Async XLA Ops:
  110.8 3.1 %copy-start = (f32[128,256]{1,0:T(8,128)S(1)}, f32[128,256]{1,0:T(8,128)}, u32[]{:S(2)}) copy-start(f32[128,256]{1,0:T(8,128)} %get-tuple-element.5) | copy-start | bytes 393220

commit v3 on v2

--- a/solution.py
+++ b/solution.py
@@ -259,7 +259,7 @@
         first = (place.order[k] * 2 + y) * pair
         return pl.ds(pl.multiple_of(first, pair), pair)
 
-    def make_features(span):
+    def make_features(span, halfway=None):
         def body(i, carry):
             cols = pl.ds(pl.multiple_of(i * tile, tile), tile)
             product = jnp.dot(xs[span, :], w_ref[:, cols], preferred_element_type=F32)
@@ -272,7 +272,11 @@
             feats[span, cols] = value.astype(BF16)
             return carry
 
-        lax.fori_loop(0, tiles, body, 0, unroll=True)
+        middle = tiles // 2
+        lax.fori_loop(0, middle, body, 0, unroll=True)
+        if halfway is not None:
+            halfway()
+        lax.fori_loop(middle, tiles, body, 0, unroll=True)
 
     def predict(span, factors, scatter, k, far, columns):
         part[:, :columns] = jnp.dot(feats[span, :], factors[...], preferred_element_type=F32)
@@ -293,10 +297,13 @@
 
     for k in range(zn):
         gather_x.near_half(k)
-        make_features(pair_rows(k, 0))
+
+        def halfway(k=k):
+            if k + 1 < zn:
+                gather_x.forward(k + 1)
+
+        make_features(pair_rows(k, 0), halfway)
         gather_x.cross(k)
-        if k + 1 < zn:
-            gather_x.forward(k + 1)
         predict(pair_rows(k, 0), joint, scatter1, k, 0, outs + top)
         if k:
             scatter1.merge_core(k - 1, 1)
@@ -324,10 +331,11 @@
         quad = 4 * rows
         projected = jnp.zeros((top, outs), F32)
         gather.forward(0)
+        gather.forward(1)
         for k in range(zn):
             gather.cross(k)
-            if k + 1 < zn:
-                gather.forward(k + 1)
+            if k + 2 < zn:
+                gather.forward(k + 2)
             gather.near_half(k)
             gather.far_half(k)
             span = pl.ds(pl.multiple_of(place.order[k] * quad, quad), quad)

time: 115 us -> 107 us (0.930)
  Pallas kernels: 110 us -> 103 us
    pallas_call x1, Pallas kernels: 110 us -> 103 us  [local(): pl.pallas_call(functools.partial(kernel, size, feat_dev * size), out_shap...]
where the time goes in v3:
time: 107 us
  Pallas kernels  103 us (96%)
  local copies, waits for them, and re-layouts  3.74 us (3%)
    pallas_call x1, Pallas kernels, local(): pl.pallas_call(functools.partial(kernel, size, feat_dev * size), out_shap...  103 us
    unnamed x4, local copies, waits for them, and re-layouts  3.74 us

profile of v3, /device:TPU:1, one launch (start us, length us, event | category | flops | bytes accessed | tf_op | source)
XLA Modules:
  0.0 107.3 jit_solution(13051691883572902312)
XLA Ops:
  0.6 103.0 %shard_map.86 = (f32[2048,256]{1,0:T(8,128)}, f32[128,256]{1,0:T(8,128)}) custom-call(bf16[128,512]{1,0:T(8,128)(2,1)} %x_ref.1, bf16[128,256]{1,0:T(8,128)(2,1)} %y_ref.1, bf16[512,2048]{1,0:T(8,128)(2,1)} %w_ref.1, f32[1,2048]{1,0:T(1,128)} %bitcast.2, f32[2048,256]{1,0:T(8,128)} %a_ref.1, bf16[2048,128]{1,0:T(8,128)(2,1)} %e_ref.1, f32[1,128]{1,0:T(1,128)} %bitcast.3), custom_call_target="tpu_custom_call" | custom-call | tf_op jit(solution)/shard_map/pallas_call | solution.py:415
  103.6 0.0 copy-start
  103.6 3.1 %copy.11 = f32[2048,256]{1,0:T(8,128)} copy(f32[2048,256]{1,0:T(8,128)} %get-tuple-element.4) | data formatting | bytes 4194304
  106.7 0.0 copy-done
  106.7 0.7 copy.12
Async XLA Ops:
  103.6 3.1 %copy-start = (f32[128,256]{1,0:T(8,128)S(1)}, f32[128,256]{1,0:T(8,128)}, u32[]{:S(2)}) copy-start(f32[128,256]{1,0:T(8,128)} %get-tuple-element.5) | copy-start | bytes 393220
